TPU v7x, 32 devices: a whole 2x2x4 slice. The times are simulated.
32 devices in a mesh: batch: 8 (over y, x, core), seq: 4 (over z).
Axes of the slice: x: 2, y: 2, z: 4, core: 2. Of those that a mesh axis runs over, the one named last changes fastest.
Arguments:
- hidden_in: bfloat16 [32, 512, 768], P('batch', 'seq'), may hold values from -6 to 6
- segment_ids: int32 [32, 512], P('batch'), may hold values from 0 to 3, as said below
- pad_mask: int32 [32, 512], P('batch'), may hold values from 0 to 1, as said below
- cotangent: bfloat16 [32, 512, 768], P('batch', 'seq'), may hold values from -6 to 6
- w_query: bfloat16 [768, 768], P(('batch', 'seq')), may hold values from -0.21875 to 0.21875
- bias_query: bfloat16 [768], P(('batch', 'seq')), may hold values from -3 to 3
- w_key: bfloat16 [768, 768], P(('batch', 'seq')), may hold values from -0.21875 to 0.21875
- w_value: bfloat16 [768, 768], P(('batch', 'seq')), may hold values from -0.21875 to 0.21875
- bias_value: bfloat16 [768], P(('batch', 'seq')), may hold values from -3 to 3
- w_out: bfloat16 [768, 768], P(('batch', 'seq')), may hold values from -1.75 to 1.75
- bias_out: bfloat16 [768], P(('batch', 'seq')), may hold values from -3 to 3
- gain_attn: bfloat16 [768], P(('batch', 'seq')), may hold values from 0.5 to 1.5
- shift_attn: bfloat16 [768], P(('batch', 'seq')), may hold values from -3 to 3
- w_up: bfloat16 [768, 3072], P(('batch', 'seq')), may hold values from -0.21875 to 0.21875
- bias_up: bfloat16 [3072], P(('batch', 'seq')), may hold values from -3 to 3
- w_down: bfloat16 [3072, 768], P(('batch', 'seq')), may hold values from -0.109375 to 0.109375
- bias_down: bfloat16 [768], P(('batch', 'seq')), may hold values from -3 to 3
- gain_ffn: bfloat16 [768], P(('batch', 'seq')), may hold values from 0.5 to 1.5
- shift_ffn: bfloat16 [768], P(('batch', 'seq')), may hold values from -3 to 3
Outputs:
- block_out: bfloat16 [32, 512, 768], P('batch', 'seq')
- grad_in: bfloat16 [32, 512, 768], P('batch', 'seq')
- grad_w_query: float32 [768, 768], P(('batch', 'seq'))
- grad_bias_query: float32 [768], P(('batch', 'seq'))
- grad_w_key: float32 [768, 768], P(('batch', 'seq'))
- grad_w_value: float32 [768, 768], P(('batch', 'seq'))
- grad_bias_value: float32 [768], P(('batch', 'seq'))
- grad_w_out: float32 [768, 768], P(('batch', 'seq'))
- grad_bias_out: float32 [768], P(('batch', 'seq'))
- grad_gain_attn: float32 [768], P(('batch', 'seq'))
- grad_shift_attn: float32 [768], P(('batch', 'seq'))
- grad_w_up: float32 [768, 3072], P(('batch', 'seq'))
- grad_bias_up: float32 [3072], P(('batch', 'seq'))
- grad_w_down: float32 [3072, 768], P(('batch', 'seq'))
- grad_bias_down: float32 [768], P(('batch', 'seq'))
- grad_gain_ffn: float32 [768], P(('batch', 'seq'))
- grad_shift_ffn: float32 [768], P(('batch', 'seq'))
Inputs may be any that keep to these rules, and one draw needn't show every extreme that they name: `segment_ids`: along each row the document numbers never fall and start at 0; a row holds at most four documents; every document begins with a real token; in the rows of each index of batch at least one row is a single document and another holds exactly four. `pad_mask`: Padding, where a row has any, is a tail of the row that lies inside the row's last document, at most 128 positions long.
All inputs are finite; a program needn't handle non-finite values.
Results may differ from a plain program's by a relative error of at most 0.015.
Values may be sent and summed in bfloat16 or wider, within the bound.
A program may use at most 256 MiB of HBM per device.

v0:
```python
import jax
import jax.numpy as jnp
from jax import lax
from jax.experimental import pallas as pl
from jax.experimental.pallas import tpu as pltpu
from jax.sharding import PartitionSpec as P

BF = jnp.bfloat16
F32 = jnp.float32
MESH = pl.DeviceIdType.MESH
EPS = 1e-5
NEG = -1e9
C0 = 0.7978845608028654
C1 = 0.044715
NN = (((1,), (0,)), ((), ()))
NT = (((1,), (1,)), ((), ()))
TN = (((0,), (0,)), ((), ()))
VMEM = pltpu.VMEM
ANY = pl.ANY
ROW_BQ, ROW_BV, ROW_BO, ROW_GA, ROW_SA, ROW_BD, ROW_GF, ROW_SF, ROW_UP = 0, 2, 3, 4, 5, 6, 7, 8, 9
VROWS = 16


def dg(a, b, dims):
    return lax.dot_general(a, b, dims, preferred_element_type=F32)


def ds(start, size):
    return pl.ds(pl.multiple_of(start, size), size)


class Place:
    def __init__(self, fold):
        bidx = lax.axis_index("batch")
        z = lax.axis_index("seq")
        hi = bidx // fold
        lo = bidx % fold
        y = hi // 4
        x = (hi // 2) % 2
        c = hi % 2
        self.y, self.x, self.c, self.z, self.b = y, x, c, z, hi
        self.k = hi * 4 + z
        self.bx = y * 4 + (1 - x) * 2 + c
        self.by = (1 - y) * 4 + x * 2 + c
        self.bd = (1 - y) * 4 + (1 - x) * 2 + c
        self.bc = y * 4 + x * 2 + (1 - c)

        def dev(block):
            return (block * fold + lo, z)

        self.xdev, self.ydev, self.cdev = dev(self.bx), dev(self.by), dev(self.bc)
        self.zidx = [z + 1 - 2 * (z % 2), z + 2 - 4 * (z // 2), 3 - z]
        self.zfrom = self.zidx
        self.zdev = [(bidx, zi) for zi in self.zidx]
        self.zp = z + 1 - 2 * (z % 2)
        self.inner = (z == 1) | (z == 2)
        self.outer = (z == 0) | (z == 3)
        self.zm = 3 - z
        self.pdev, self.mdev = (bidx, self.zp), (bidx, self.zm)

    def greet(self):
        bar = pltpu.get_barrier_semaphore()
        for d in [self.xdev, self.ydev, self.cdev] + self.zdev:
            pl.semaphore_signal(bar, inc=1, device_id=d, device_id_type=MESH)
        pl.semaphore_wait(bar, 6)


class Wire:
    def __init__(self, send_sems, recv_sems):
        self.ss, self.rs, self.n, self.open, self.cond = send_sems, recv_sems, 0, [], None

    def when(self, cond, body):
        @pl.when(cond)
        def _():
            self.cond = cond
            body()
            self.cond = None

    def send(self, src, dst, device):
        i = self.n
        self.n += 1

        def make():
            return pltpu.make_async_remote_copy(src_ref=src(), dst_ref=dst(), send_sem=self.ss.at[i], recv_sem=self.rs.at[i],
                                                device_id=device, device_id_type=MESH)

        make().start()
        tag = (i, device, make, self.cond)
        self.open.append(tag)
        return tag

    def recv(self, tag, dst):
        i, device = tag[:2]
        pltpu.make_async_remote_copy(src_ref=dst, dst_ref=dst, send_sem=self.ss.at[i], recv_sem=self.rs.at[i],
                                     device_id=device, device_id_type=MESH).wait_recv()

    def sent(self, tag):
        tag[2]().wait_send()
        self.open = [other for other in self.open if other is not tag]

    def finish(self):
        for tag in self.open:
            if tag[3] is None:
                tag[2]().wait_send()
            else:
                pl.when(tag[3])(lambda tag=tag: tag[2]().wait_send())
        self.open = []


class Local:
    def __init__(self, sems):
        self.sems, self.n, self.open = sems, 0, []

    def start(self, src, dst):
        i = self.n
        self.n += 1

        def make():
            return pltpu.make_async_copy(src(), dst(), self.sems.at[i])

        make().start()
        self.open.append(make)
        return make

    def wait(self, make):
        make().wait()
        self.open = [other for other in self.open if other is not make]

    def finish(self):
        for make in self.open:
            make().wait()
        self.open = []


def norm_rows(v, gain, shift):
    center = v - jnp.mean(v, axis=-1, keepdims=True)
    inv = lax.rsqrt(jnp.mean(center * center, axis=-1, keepdims=True) + EPS)
    xhat = center * inv
    return xhat * gain + shift, xhat, inv


def norm_back(g, xhat, inv, gain):
    e = g * gain
    return inv * (e - jnp.mean(e, axis=-1, keepdims=True) - xhat * jnp.mean(e * xhat, axis=-1, keepdims=True))


def rows_sum(v):
    return jnp.sum(v, axis=0, keepdims=True)


def place_matrix(rows, width, start, count):
    i = lax.broadcasted_iota(jnp.int32, (rows, width), 0)
    j = lax.broadcasted_iota(jnp.int32, (rows, width), 1)
    return jnp.where((j == start + i) & (i < count), 1.0, 0.0).astype(BF)


def segments(seg_ref, pad_ref, z, length):
    seg = seg_ref[pl.ds(z, 1), :].astype(F32)
    live = pad_ref[pl.ds(z, 1), :]
    keyed = jnp.where(live == 1, seg, -1.0)

    def column(row):
        return jnp.broadcast_to(row, (128, length)).T[:, 0:1]

    return seg, keyed, column


def forward_kernel(fold, T, D, FF, r, rd,
                   hidden, cot, seg, pad, wq, wk, wv, wo, wu, wd,
                   v0, v1, v2, v3, v4, v5, v6, v7, v8,
                   o_tok, o_qkv, o_att, o_lse, o_nlow, o_xh1, o_inv1, o_act, o_gp, o_gmid, o_gffn, o_out, o_vec,
                   o_gvec, o_wA, o_wU, o_wD,
                   zA, zU, wA, wU, wD, tok, cotr, qkv, att, lse, nlow, xh1, inv1, normed, act, gp, tmp, gffn, out,
                   vec, gvec, table, vsend, vland, ss, rs, ls):
    me = Place(fold)
    wire = Wire(ss, rs)
    local = Local(ls)
    z, b = me.z, me.b
    Q = T // 4
    block, dblock = 4 * r, 4 * rd

    def drow(k, sub):
        return wD.at[k // 2, ds((k % 2) * dblock + sub * rd, rd)]

    def dhalf(k, sub, cols):
        return wD.at[k // 2, ds((k % 2) * dblock + sub * rd, rd), cols]

    own = [local.start(lambda w=w: w, lambda i=i: zA.at[i, z]) for i, w in enumerate((wq, wk, wv, wo))]
    own_u = local.start(lambda: wu, lambda: zU.at[z])
    own_d = local.start(lambda: wd, lambda: drow(b, z))
    own_t = local.start(lambda: hidden.at[z], lambda: tok.at[ds(z * Q, Q)])
    own_c = local.start(lambda: cot.at[z], lambda: cotr.at[ds(z * Q, Q)])

    table[...] = jnp.zeros_like(table)
    for i, ref in zip((ROW_BQ, ROW_BV, ROW_BO, ROW_GA, ROW_SA, ROW_BD, ROW_GF, ROW_SF, ROW_UP), (v0, v1, v2, v3, v4, v5, v6, v7, v8)):
        table[i:i + 1, 0:ref.shape[1]] = ref[...].astype(F32)
    given = table[...].astype(BF)
    v_a = dg(given, place_matrix(128, D, me.k * r, r), NN)
    per_row = D // block
    v_u = dg(given, place_matrix(128, D, (me.k % per_row) * block, block), NN)[ROW_UP:ROW_UP + 1]
    ri = lax.broadcasted_iota(jnp.int32, (VROWS, D), 0)
    up_row = ROW_UP + me.k // per_row
    vsend[0] = jnp.where(ri < ROW_UP, v_a, jnp.where(ri == up_row, jnp.broadcast_to(v_u, (VROWS, D)), 0.0)).astype(BF)

    me.greet()

    def zsend(src, dst):
        return [wire.send(lambda k=k: src(k), dst, me.zdev[k]) for k in range(3)]

    def zrecv(tags, dst):
        for k in range(3):
            wire.recv(tags[k], dst(k))

    class Spread:
        def __init__(self, region):
            self.region = region

        def go(self, k, half, n, device):
            return wire.send(lambda: self.region(k, half, n), lambda: self.region(k, half, n), device)

        def own(self):
            self.tx = self.go(b, 0, 2, me.xdev)
            self.ty = self.go(b, 0, 2, me.ydev)
            self.tc = [self.go(b, 0, 2, me.cdev)]

        def mid(self):
            g = self.region
            wire.recv(self.tx, g(me.bx, 0, 2))
            self.f1 = self.go(me.bx, 0, 1, me.ydev)
            wire.recv(self.ty, g(me.by, 0, 2))
            self.f2 = self.go(me.by, 1, 1, me.xdev)
            self.tc.append(self.go(me.bx, 0, 2, me.cdev))
            self.tc.append(self.go(me.by, 0, 2, me.cdev))

        def last(self):
            g = self.region
            wire.recv(self.f1, g(me.bd, 0, 1))
            wire.recv(self.f2, g(me.bd, 1, 1))
            self.tc.append(self.go(me.bd, 0, 2, me.cdev))

        def done(self):
            for tag, k in zip(self.tc, (me.b, me.bx, me.by, me.bd)):
                wire.recv(tag, self.region(k + 1 - 2 * me.c, 0, 2))

    def part(k, half, n, size):
        h = size // 2
        return ds(k * size + half * h, h) if n == 1 else ds(k * size, size)

    hF, hD = FF // 2, D // 2
    s_qkv = Spread(lambda k, half, n: wA.at[0:3, part(k, half, n, block)])
    s_o = Spread(lambda k, half, n: wA.at[3, part(k, half, n, block)])
    s_u = [Spread(lambda k, half, n, i=i: wU.at[part(k, half, n, block), i * hF:(i + 1) * hF]) for i in range(2)]
    s_d = [Spread(lambda k, half, n, i=i: wD.at[k // 2, part(k % 2, half, n, dblock), i * hD:(i + 1) * hD]) for i in range(2)]


    def join(parts):
        return jnp.concatenate([p.astype(F32) for p in parts], axis=0).astype(BF)

    t_vec = [wire.send(lambda: vsend.at[0], lambda k=k: vland.at[k], me.zdev[k]) for k in range(3)]
    for cp in own[:3]:
        local.wait(cp)
    t_qkv = zsend(lambda k: zA.at[0:3, z], lambda: zA.at[0:3, z])
    t_u = zsend(lambda k: wu, lambda: zU.at[z])
    t_hid = zsend(lambda k: hidden.at[me.zidx[k]], lambda: tok.at[ds(z * Q, Q)])
    local.wait(own[3])
    t_o = zsend(lambda k: zA.at[3, z], lambda: zA.at[3, z])
    halves = [slice(0, hD), slice(hD, D)]
    t_d = [zsend(lambda k, h=h: wd.at[:, h], lambda h=h: dhalf(b, z, h)) for h in halves]

    zrecv(t_vec, lambda k: vland.at[k])
    vsend[1] = vsend[0] + vland[0] + vland[1] + vland[2]
    tv = wire.send(lambda: vsend.at[1], lambda: vland.at[3], me.xdev)

    zrecv(t_qkv, lambda k: zA.at[0:3, me.zfrom[k]])
    for i in range(3):
        wA[i, ds(b * block, block), :] = join([zA[i, s] for s in range(4)])
    s_qkv.own()
    wire.recv(tv, vland.at[3])
    vsend[2] = vsend[1] + vland[3]
    tv = wire.send(lambda: vsend.at[2], lambda: vland.at[4], me.ydev)
    s_qkv.mid()
    wire.recv(tv, vland.at[4])
    vsend[3] = vsend[2] + vland[4]
    tv = wire.send(lambda: vsend.at[3], lambda: vland.at[5], me.cdev)
    local.wait(own_u)
    zrecv(t_u, lambda k: zU.at[me.zfrom[k]])
    wU[ds(b * block, block), :] = join([zU[s] for s in range(4)])
    s_u[0].own()
    s_u[1].own()
    s_qkv.last()
    wire.recv(tv, vland.at[5])
    vec[...] = vsend[3].astype(F32) + vland[5].astype(F32)
    local.start(lambda: vec, lambda: o_vec)
    s_qkv.done()
    s_u[0].mid()
    local.wait(own_t)
    zrecv(t_hid, lambda k: tok.at[ds(me.zfrom[k] * Q, Q)])
    local.start(lambda: tok, lambda: o_tok)

    def project(j):
        v = dg(tok[...], wA[j], NN) + vec[pl.ds(j, 1), :]
        v = v.astype(BF)
        qkv[j] = v * jnp.where(j == 0, 0.125, 1.0).astype(BF)

    pl.loop(0, 3)(project)
    local.start(lambda: qkv, lambda: o_qkv)
    s_u[1].mid()
    zrecv(t_o, lambda k: zA.at[3, me.zfrom[k]])
    wA[3, ds(b * block, block), :] = join([zA[3, s] for s in range(4)])
    s_o.own()

    seg_row, key_row, column = segments(seg, pad, z, T)
    seg_col = column(seg_row)
    lane = lax.broadcasted_iota(jnp.int32, (T, 128), 1)
    lo = lane < 64

    def attend(p):
        o = ds(p * 128, 128)
        k = qkv[1, :, o]
        v = qkv[2, :, o]
        one = jnp.ones_like(v)
        zero = jnp.zeros_like(v)
        v0_, v1_ = jnp.where(lo, v, one), jnp.where(lo, one, v)
        k0, k1 = jnp.where(lo, k, zero), jnp.where(lo, zero, k)
        for step in range(T // 128):
            rows = slice(step * 128, (step + 1) * 128)
            q = qkv[0, rows, o]
            ok = seg_col[rows] == key_row
            res, top = [], []
            for kk, vv in ((k0, v0_), (k1, v1_)):
                s = jnp.where(ok, dg(q, kk, NT), NEG)
                m = jnp.max(s, axis=-1, keepdims=True)
                res.append(dg(jnp.exp(s - m).astype(BF), vv, NN))
                top.append(m)
            low = lo[:128]
            num = jnp.where(low, res[0], res[1])
            den = pltpu.roll(jnp.where(low, res[1], res[0]), 64, 1)
            att[rows, o] = (num / den).astype(BF)
            lt = (jnp.log(den) + jnp.where(low, top[0], top[1])).T
            lse[p, 0:1, rows] = lt[0:1]
            lse[p, 1:2, rows] = lt[64:65]

    tags = {}

    def serve0():
        s_u[0].last()

    def serve1():
        pass

    def serve2():
        local.wait(own_d)
        zrecv(t_d[0], lambda k: dhalf(b, me.zfrom[k], halves[0]))
        s_d[0].own()
        s_o.mid()

    def serve3():
        s_u[1].last()

    def serve4():
        zrecv(t_d[1], lambda k: dhalf(b, me.zfrom[k], halves[1]))
        s_d[1].own()
        tags["cot"] = zsend(lambda k: cot.at[me.zidx[k]], lambda: cotr.at[ds(z * Q, Q)])
        s_o.last()

    def serve5():
        s_d[0].mid()

    services = [serve0, serve1, serve2, serve3, serve4, serve5]

    @pl.loop(0, 6)
    def _(p):
        attend(p)
        for i, service in enumerate(services):
            pl.when(p == i)(service)

    local.start(lambda: att, lambda: o_att)
    local.start(lambda: lse, lambda: o_lse)
    s_o.done()
    local.start(lambda: wA, lambda: o_wA)
    tmp[...] = dg(att[...], wA[3], NN) + vec[ROW_BO:ROW_BO + 1, :]

    def norm_one(i):
        rr = ds(i * 64, 64)
        y_, xh, inv = norm_rows(tmp[rr, :] + tok[rr, :].astype(F32), vec[ROW_GA:ROW_GA + 1, :], vec[ROW_SA:ROW_SA + 1, :])
        normed[rr, :] = y_
        nlow[rr, :] = y_.astype(BF)
        xh1[rr, :] = xh
        inv1[rr, :] = jnp.broadcast_to(inv, (64, 128))

    pl.loop(0, T // 64)(norm_one)
    local.start(lambda: nlow, lambda: o_nlow)
    local.start(lambda: xh1, lambda: o_xh1)
    local.start(lambda: inv1, lambda: o_inv1)
    s_u[0].done()
    s_u[1].done()
    local.start(lambda: wU, lambda: o_wU)

    wide = D // 2

    def up(j):
        o = ds(j * wide, wide)
        bias = vec[pl.ds(ROW_UP + j // 2, 1), ds((j % 2) * wide, wide)]
        v = dg(nlow[...], wU[:, o], NN) + bias
        v2 = v * v
        t = jnp.tanh(v * (C0 + C0 * C1 * v2))
        half = 0.5 * (1 + t)
        act[:, o] = (v * half).astype(BF)
        gp[:, o] = (half + 0.5 * v * (1 - t * t) * (C0 + 3 * C0 * C1 * v2)).astype(BF)

    @pl.loop(0, FF // wide)
    def _(j):
        up(j)
        pl.when(j == 2)(s_d[1].mid)

    local.start(lambda: act, lambda: o_act)
    local.start(lambda: gp, lambda: o_gp)
    s_d[0].last()
    s_d[1].last()
    s_d[0].done()
    s_d[1].done()
    local.start(lambda: wD, lambda: o_wD)

    tmp[...] = dg(act[:, 0:D], wD[0], NN) + vec[ROW_BD:ROW_BD + 1, :]

    def down(j):
        tmp[...] += dg(act[:, ds(j * D, D)], wD[j], NN)

    pl.loop(1, FF // D)(down)
    local.wait(own_c)
    zrecv(tags["cot"], lambda k: cotr.at[ds(me.zfrom[k] * Q, Q)])
    zero_row = jnp.zeros((1, D), F32)
    gvec[...] = jnp.zeros_like(gvec)

    def norm_two(i, sums):
        rr = ds(i * 64, 64)
        gain = vec[ROW_GF:ROW_GF + 1, :]
        y_, xh, inv = norm_rows(tmp[rr, :] + normed[rr, :], gain, vec[ROW_SF:ROW_SF + 1, :])
        out[rr, :] = y_.astype(BF)
        g = cotr[rr, :].astype(F32)
        gm = norm_back(g, xh, inv, gain)
        gl = gm.astype(BF)
        tmp[rr, :] = gm
        gffn[rr, :] = gl
        return sums[0] + rows_sum(g * xh), sums[1] + rows_sum(g), sums[2] + rows_sum(gl.astype(F32))

    s0, s1, s2 = lax.fori_loop(0, T // 64, norm_two, (zero_row, zero_row, zero_row))
    gvec[ROW_GF:ROW_GF + 1, :] = s0
    gvec[ROW_SF:ROW_SF + 1, :] = s1
    gvec[ROW_BD:ROW_BD + 1, :] = s2
    local.start(lambda: gffn, lambda: o_gffn)
    local.start(lambda: out, lambda: o_out)
    local.start(lambda: tmp, lambda: o_gmid)
    local.start(lambda: gvec, lambda: o_gvec)
    wire.finish()
    local.finish()


def backward_kernel(fold, T, D, FF, r, rd, refs):
    take = iter(refs)

    def some(n):
        return [next(take) for _ in range(n)]

    (seg, pad, i_tok, i_qkv, i_att, i_lse, i_nlow, i_xh1, i_inv1, i_act, i_gp, i_gmid, i_gffn, i_out,
     i_vec, i_gvec, i_wA, i_wU, i_wD) = some(19)
    bout, gin_out, gA_out, gU_out, gD_out, gv_out = some(6)
    (w1, wU, tok, qkv, att, lse, nlow, xh1, inv1, act, gp, gmid, gffn, vec, gvec, gattn, gatt, gqkv) = some(18)
    d_snd0, d_snd1, u_snd, o_snd, a_snd = some(5)
    mines, ones, firsts, seconds, outs, ins = [some(8) for _ in range(6)]
    vsend, vland, ss, rs, ls = some(5)

    me = Place(fold)
    wire = Wire(ss, rs)
    local = Local(ls)
    z, b, c, x, y = me.z, me.b, me.c, me.x, me.y
    Q = T // 4

    def load(src, dst):
        return local.start(lambda: src, lambda: dst)

    l_act, l_gffn, l_wD, l_gp = load(i_act, act), load(i_gffn, gffn), load(i_wD, w1), load(i_gp, gp)
    l_gvec, l_nlow, l_gmid, l_wU = load(i_gvec, gvec), load(i_nlow, nlow), load(i_gmid, gmid), load(i_wU, wU)
    l_vec, l_xh1, l_inv1, l_att = load(i_vec, vec), load(i_xh1, xh1), load(i_inv1, inv1), load(i_att, att)
    l_qkv, l_lse, l_tok = load(i_qkv, qkv), load(i_lse, lse), load(i_tok, tok)
    local.start(lambda: i_out.at[ds(z * Q, Q)], lambda: bout.at[z])
    me.greet()
    t_out = [wire.send(lambda k=k: i_out.at[ds(me.zidx[k] * Q, Q)], lambda: bout.at[z], me.zdev[k]) for k in range(3)]

    def keep(v0, v1):
        first = c == 0
        return jnp.where(first, v0, v1).astype(BF), jnp.where(first, v1, v0).astype(BF)

    def plus(a, e):
        return (a.astype(F32) + e.astype(F32)).astype(BF)

    class Sum:
        def __init__(self, i, snd, rows, line, write):
            self.snd, self.rows, self.line, self.write = snd, rows, line, write
            self.mine, self.r1, self.ra, self.rb, self.zs, self.zr = (mines[i], ones[i], firsts[i], seconds[i], outs[i], ins[i])

        def core(self):
            self.tc = wire.send(lambda: self.snd, lambda: self.r1, me.cdev)

        def plane_one(self):
            n = 2 * self.rows
            wire.recv(self.tc, self.r1)

            @pl.loop(0, 2)
            def _(i):
                for j in range(2):
                    self.mine[i, j] = plus(self.mine[i, j], self.r1[i, j])

            self.tx = wire.send(lambda: self.mine.at[:, 1 - x, 0:n], lambda: self.ra.at[0], me.xdev)
            self.ty = wire.send(lambda: self.mine.at[1 - y, :, n:2 * n], lambda: self.ra.at[1], me.ydev)

        def plane_two(self):
            n = 2 * self.rows
            wire.recv(self.tx, self.ra.at[0])
            for i in range(2):
                self.mine[i, x, 0:n] = plus(self.mine[i, x, 0:n], self.ra[0, i])
            self.ty2 = wire.send(lambda: self.mine.at[1 - y, x, 0:n], lambda: self.rb.at[0], me.ydev)
            wire.recv(self.ty, self.ra.at[1])
            for i in range(2):
                self.mine[y, i, n:2 * n] = plus(self.mine[y, i, n:2 * n], self.ra[1, i])
            self.tx2 = wire.send(lambda: self.mine.at[y, 1 - x, n:2 * n], lambda: self.rb.at[1], me.xdev)

        def along(self):
            n = 2 * self.rows
            q = self.rows
            for half, tag in ((0, self.ty2), (1, self.tx2)):
                wire.recv(tag, self.rb.at[half])
                v = self.mine[y, x, half * n:(half + 1) * n].astype(F32) + self.rb[half].astype(F32)
                self.zs[2 * half] = v[0:q].astype(BF)
                self.zs[2 * half + 1] = v[q:2 * q].astype(BF)
            if self.line:
                def outer():
                    self.t1 = wire.send(lambda: self.zs.at[pl.ds(jnp.where(z == 0, 1, 0), 3)], lambda: self.zr.at[0:3], me.pdev)

                wire.when(me.outer, outer)
            else:
                self.tz = [wire.send(lambda k=k: self.zs.at[me.zidx[k]], lambda k=k: self.zr.at[k], me.zdev[k]) for k in range(3)]

        def line_one(self):
            def inner():
                wire.recv(self.t1, self.zr.at[0:3])
                base = jnp.where(z == 1, 1, 0)
                start = jnp.where(z == 1, 2, 0)
                for i in range(2):
                    self.zs[start + i] = plus(self.zs[start + i], self.zr[start + i - base])
                self.t2 = wire.send(lambda: self.zs.at[pl.ds(jnp.where(z == 1, 2, 0), 2)], lambda: self.zr.at[3:5], me.mdev)

            wire.when(me.inner, inner)

        def line_two(self):
            def inner():
                wire.recv(self.t2, self.zr.at[3:5])
                base = jnp.where(z == 1, 1, 0)
                pair = jnp.where(z == 1, 0, 2)
                self.zs[me.zp] = plus(self.zs[me.zp], self.zr[3 + me.zp - pair])
                self.t3 = wire.send(lambda: self.zs.at[me.zp], lambda: self.zr.at[0], me.pdev)
                self.write(self.zs[z].astype(F32) + self.zr[z - base].astype(F32) + self.zr[3 + z - pair].astype(F32))

            wire.when(me.inner, inner)

        def done(self):
            if self.line:
                def outer():
                    wire.recv(self.t3, self.zr.at[0])
                    self.write(self.zs[z].astype(F32) + self.zr[0].astype(F32))

                wire.when(me.outer, outer)
            else:
                v = self.zs[z].astype(F32)
                for k in range(3):
                    wire.recv(self.tz[k], self.zr.at[k])
                    v = v + self.zr[k].astype(F32)
                self.write(v)

    third, hF, hD = D // 3, FF // 2, D // 2

    def write_d(i):
        def f(v):
            gD_out[:, i * third:(i + 1) * third] = v
        return f

    def write_u(i):
        def f(v):
            gU_out[:, i * hF:(i + 1) * hF] = v
        return f

    def write_o(v):
        gA_out[3] = v

    def write_a(i):
        def f(v):
            for m in range(3):
                gA_out[m, :, i * hD:(i + 1) * hD] = v[:, m * hD:(m + 1) * hD]
        return f

    D0 = Sum(0, d_snd0, rd, False, write_d(0))
    D1 = Sum(1, d_snd1, rd, False, write_d(1))
    D2 = Sum(2, d_snd0, rd, False, write_d(2))
    U0 = Sum(3, u_snd, r, False, write_u(0))
    U1 = Sum(4, u_snd, r, True, write_u(1))
    O = Sum(5, o_snd, r, False, write_o)
    A0 = Sum(6, a_snd, r, False, write_a(0))
    A1 = Sum(7, a_snd, r, False, write_a(1))

    def down_grad(part, i):
        cols = slice(i * third, (i + 1) * third)

        @pl.loop(0, 4)
        def _(i):
            v = dg(act[:, ds(i * D, D)], gffn[:, cols], TN)
            mine, theirs = keep(v[0:4 * rd], v[4 * rd:8 * rd])
            part.mine[i // 2, i % 2] = mine
            part.snd[i // 2, i % 2] = theirs

    def store(part, v, cols):
        n = 4 * r
        for i in range(4):
            mine, theirs = keep(v[(2 * i) * n:(2 * i + 1) * n], v[(2 * i + 1) * n:(2 * i + 2) * n])
            part.mine[i // 2, i % 2, :, cols] = mine
            part.snd[i // 2, i % 2, :, cols] = theirs

    def inner(j):
        o = ds(j * D, D)
        gi = (dg(gffn[...], w1[j], NT) * gp[:, o].astype(F32)).astype(BF)
        gp[:, o] = gi
        gvec[pl.ds(ROW_UP + j, 1), :] = rows_sum(gi.astype(F32))

    def up_grad(part, first):
        wide = hF // 3

        @pl.loop(0, 3)
        def _(j):
            o = ds(j * wide, wide)
            store(part, dg(nlow[...], gp[:, ds(first + j * wide, wide)], TN), o)

    local.wait(l_act)
    local.wait(l_gffn)
    down_grad(D0, 0)
    D0.core()
    down_grad(D1, 1)
    D1.core()
    D0.plane_one()
    wire.sent(D0.tc)
    down_grad(D2, 2)
    D2.core()
    D1.plane_one()
    local.wait(l_wD)
    local.wait(l_gp)
    local.wait(l_gvec)
    pl.loop(0, FF // D)(inner)
    l_wA = load(i_wA, w1)
    D0.plane_two()
    D2.plane_one()
    local.wait(l_wU)
    local.wait(l_gmid)
    gmid[...] += dg(gp[...], wU[...], NT)
    local.wait(l_vec)
    local.wait(l_xh1)
    local.wait(l_inv1)
    zero_row = jnp.zeros((1, D), F32)

    def norm_one(i, sums):
        rr = ds(i * 64, 64)
        g = gmid[rr, :]
        xh = xh1[rr, :]
        gm = norm_back(g, xh, inv1[rr, 0:1], vec[ROW_GA:ROW_GA + 1, :])
        gl = gm.astype(BF)
        gmid[rr, :] = gm
        gattn[rr, :] = gl
        return sums[0] + rows_sum(g * xh), sums[1] + rows_sum(g), sums[2] + rows_sum(gl.astype(F32))

    s0, s1, s2 = lax.fori_loop(0, T // 64, norm_one, (zero_row, zero_row, zero_row))
    gvec[ROW_GA:ROW_GA + 1, :] = s0
    gvec[ROW_SA:ROW_SA + 1, :] = s1
    gvec[ROW_BO:ROW_BO + 1, :] = s2
    D1.plane_two()
    local.wait(l_nlow)
    up_grad(U0, 0)
    U0.core()
    local.wait(l_att)
    local.wait(l_wA)
    gatt[...] = dg(gattn[...], w1[3], NT).astype(BF)
    local.wait(l_qkv)
    local.wait(l_lse)
    local.wait(l_tok)

    seg_row, key_row, column = segments(seg, pad, z, T)
    key_col = column(key_row)
    lane = lax.broadcasted_iota(jnp.int32, (T, 128), 1)
    lo = lane < 64
    pick = (lax.broadcasted_iota(jnp.int32, (8, 128), 1) // 64 == lax.broadcasted_iota(jnp.int32, (8, 128), 0)).astype(BF)

    def attend(p):
        o = ds(p * 128, 128)
        q = qkv[0, :, o]
        k = qkv[1, :, o]
        g = gatt[:, o]
        prod = g.astype(F32) * att[:, o].astype(F32)
        hi = prod.astype(BF)
        rest = (prod - hi.astype(F32)).astype(BF)
        delta = dg(pick, hi, NT) + dg(pick, rest, NT)
        zero = jnp.zeros_like(q)
        qm = (jnp.where(lo, q, zero), jnp.where(lo, zero, q))
        gm = (jnp.where(lo, g, zero), jnp.where(lo, zero, g))
        km = (jnp.where(lo, k, zero), jnp.where(lo, zero, k))
        dq = jnp.zeros((T, 128), F32)
        for step in range(T // 128):
            rows = slice(step * 128, (step + 1) * 128)
            kc = qkv[1, rows, o]
            vc = qkv[2, rows, o]
            ok = key_col[rows] == seg_row
            dk = jnp.zeros((128, 128), F32)
            dv = jnp.zeros((128, 128), F32)
            for hh in range(2):
                s = jnp.where(ok, dg(kc, qm[hh], NT), NEG)
                pt = jnp.exp(s - lse[p, hh:hh + 1, :])
                dp = dg(vc, gm[hh], NT)
                dsc = (pt * (dp - delta[hh:hh + 1, :])).astype(BF)
                dv = dv + dg(pt.astype(BF), gm[hh], NN)
                dk = dk + dg(dsc, qm[hh], NN)
                dq = dq + dg(dsc, km[hh][rows], TN)
            gqkv[1, rows, o] = dk.astype(BF)
            gqkv[2, rows, o] = dv.astype(BF)
        gqkv[0, :, o] = (dq * 0.125).astype(BF)

    def qkv_grad(part, first):
        @pl.loop(0, 3)
        def _(j):
            store(part, dg(tok[...], gqkv[j, :, first:first + hD], TN), ds(j * hD, hD))

    def serve0():
        U0.plane_one()
        D2.plane_two()
        D0.along()

    def serve1():
        D1.along()
        wire.sent(U0.tc)
        up_grad(U1, hF)
        U1.core()

    def serve2():
        U1.plane_one()
        D0.done()

    def serve3():
        U0.plane_two()

    def serve4():
        D1.done()
        D2.along()

    def serve5():
        U1.plane_two()

    services = [serve0, serve1, serve2, serve3, serve4, serve5]

    @pl.loop(0, 6)
    def _(p):
        attend(p)
        for i, service in enumerate(services):
            pl.when(p == i)(service)

    gin = gattn
    store(O, dg(att[...], gattn[...], TN), slice(0, D))
    O.core()
    U0.along()
    gmid[...] += dg(gqkv[0], w1[0], NT)
    gmid[...] += dg(gqkv[1], w1[1], NT)
    gin[...] = (gmid[...] + dg(gqkv[2], w1[2], NT)).astype(BF)
    local.start(lambda: gin.at[ds(z * Q, Q)], lambda: gin_out.at[z])
    t_gin = [wire.send(lambda k=k: gin.at[ds(me.zidx[k] * Q, Q)], lambda: gin_out.at[z], me.zdev[k]) for k in range(3)]
    O.plane_one()
    qkv_grad(A0, 0)
    A0.core()
    for j, row in ((0, ROW_BQ), (2, ROW_BV)):
        gvec[row:row + 1, :] = rows_sum(gqkv[j].astype(F32))
    tv = wire.send(lambda: gvec, lambda: vland.at[0], me.cdev)
    A0.plane_one()
    wire.sent(A0.tc)
    qkv_grad(A1, hD)
    A1.core()
    D2.done()
    wire.recv(tv, vland.at[0])
    vsend[0] = gvec[...] + vland[0]
    tv = wire.send(lambda: vsend.at[0], lambda: vland.at[1], me.xdev)
    O.plane_two()
    U1.along()
    A1.plane_one()
    wire.recv(tv, vland.at[1])
    vsend[1] = vsend[0] + vland[1]
    tv = wire.send(lambda: vsend.at[1], lambda: vland.at[2], me.ydev)
    A0.plane_two()
    O.along()
    wire.recv(tv, vland.at[2])
    vsend[2] = vsend[1] + vland[2]
    tvs = [wire.send(lambda: vsend.at[2], lambda k=k: vland.at[3 + k], me.zdev[k]) for k in range(3)]
    A1.plane_two()
    U1.line_one()
    A0.along()
    A1.along()
    U0.done()
    U1.line_two()
    U1.done()
    O.done()
    total = vsend[2]
    for k in range(3):
        wire.recv(tvs[k], vland.at[3 + k])
        total = total + vland[3 + k]
    vsend[3] = total

    def exact(v, m):
        a = v.astype(BF)
        v = v - a.astype(F32)
        e = v.astype(BF)
        v = (v - e.astype(F32)).astype(BF)
        return dg(a, m, NT) + dg(e, m, NT) + dg(v, m, NT)

    per_row = D // (4 * r)
    gv = exact(total, place_matrix(128, D, me.k * r, r))
    row = vsend[3, pl.ds(ROW_UP + me.k // per_row, 1), :]
    gu = exact(jnp.broadcast_to(row, (VROWS, D)), place_matrix(128, D, (me.k % per_row) * (4 * r), 4 * r))
    ri = lax.broadcasted_iota(jnp.int32, (VROWS, 128), 0)
    gv_out[...] = jnp.where(ri < ROW_UP, gv, gu)
    A0.done()
    A1.done()
    for k in range(3):
        wire.recv(t_out[k], bout.at[me.zfrom[k]])
        wire.recv(t_gin[k], gin_out.at[me.zfrom[k]])
    wire.finish()
    local.finish()


def finish_kernel(bout, gin, gA, gU, gD, gv, o_b, o_g, o_q, o_k, o_v, o_o, o_u, o_d, *rest):
    vecs, (s_b, s_g, s_A, s_U, s_D, sems) = rest[:9], rest[9:]
    loads = [(bout, s_b), (gin, s_g), (gA, s_A), (gU, s_U), (gD, s_D)]
    loads = [pltpu.make_async_copy(src, dst, sems.at[i]) for i, (src, dst) in enumerate(loads)]
    for cp in loads:
        cp.start()
    for row, ref in zip((ROW_BQ, ROW_BV, ROW_BO, ROW_GA, ROW_SA, ROW_UP, ROW_BD, ROW_GF, ROW_SF), vecs):
        ref[...] = gv[row:row + 1, 0:ref.shape[1]]
    stores = [[(s_b, o_b)], [(s_g, o_g)], [(s_A.at[i], ref) for i, ref in enumerate((o_q, o_k, o_v, o_o))], [(s_U, o_u)], [(s_D, o_d)]]
    out, n = [], len(loads)
    for cp, group in zip(loads, stores):
        cp.wait()
        for src, dst in group:
            out.append(pltpu.make_async_copy(src, dst, sems.at[n]))
            out[-1].start()
            n += 1
    for cp in out:
        cp.wait()


def per_device(fold, hidden_in, segment_ids, pad_mask, cotangent, w_query, bias_query, w_key, w_value, bias_value,
               w_out, bias_out, gain_attn, shift_attn, w_up, bias_up, w_down, bias_down, gain_ffn, shift_ffn):
    rows, Q, D = hidden_in.shape
    T = segment_ids.shape[1]
    mats = [w_query, w_key, w_value, w_out, w_up, w_down]
    vecs = [bias_query, bias_value, bias_out, gain_attn, shift_attn, bias_down, gain_ffn, shift_ffn, bias_up]
    hi = lax.axis_index("batch") // fold
    part = hi * 4 + lax.axis_index("seq")
    if fold > 1:
        def widen(w):
            whole = lax.all_gather(w, ("batch", "seq"), axis=0, tiled=True)
            n = w.shape[0] * fold
            return lax.dynamic_slice_in_dim(whole, part * n, n, 0)
        mats = [widen(w) for w in mats]
        vecs = [widen(v) for v in vecs]
    wq, wk, wv, wo, wu, wd = mats
    r, rd, FF = wq.shape[0], wd.shape[0], wu.shape[1]

    def shape(s, d=BF):
        return jax.ShapeDtypeStruct(s, d)

    any_spec = pl.BlockSpec(memory_space=ANY)
    vm_spec = pl.BlockSpec(memory_space=VMEM)
    saved = [shape((T, D)), shape((3, T, D)), shape((T, D)), shape((6, 8, T), F32), shape((T, D)), shape((T, D), F32),
             shape((T, 128), F32), shape((T, FF)), shape((T, FF)), shape((T, D), F32), shape((T, D)), shape((T, D)),
             shape((VROWS, D), F32), shape((VROWS, D), F32), shape((4, D, D)), shape((D, FF)), shape((4, D, D))]
    n_remote = 112
    sems = [pltpu.SemaphoreType.DMA((n_remote,)), pltpu.SemaphoreType.DMA((n_remote,)), pltpu.SemaphoreType.DMA((32,))]
    fwd = pl.pallas_call(
        lambda *refs: forward_kernel(fold, T, D, FF, r, rd, *refs),
        name="forward",
        out_shape=saved,
        in_specs=[any_spec, any_spec, vm_spec, vm_spec] + [any_spec] * 6 + [vm_spec] * 9,
        out_specs=[any_spec] * len(saved),
        scratch_shapes=[
            VMEM((4, 4, r, D), BF), VMEM((4, r, FF), BF), VMEM((4, D, D), BF), VMEM((D, FF), BF), VMEM((4, D, D), BF),
            VMEM((T, D), BF), VMEM((T, D), BF), VMEM((3, T, D), BF), VMEM((T, D), BF), VMEM((6, 8, T), F32),
            VMEM((T, D), BF), VMEM((T, D), F32), VMEM((T, 128), F32), VMEM((T, D), F32), VMEM((T, FF), BF),
            VMEM((T, FF), BF), VMEM((T, D), F32), VMEM((T, D), BF), VMEM((T, D), BF),
            VMEM((VROWS, D), F32), VMEM((VROWS, D), F32), VMEM((VROWS, 128), F32), VMEM((4, VROWS, D), BF),
            VMEM((6, VROWS, D), BF),
        ] + sems,
        compiler_params=pltpu.CompilerParams(collective_id=0, has_side_effects=True, vmem_limit_bytes=58 * 2**20),
    )
    kept = fwd(hidden_in, cotangent, segment_ids, pad_mask, wq, wk, wv, wo, wu, wd, *[v.reshape(1, -1) for v in vecs])

    parts = [(4 * rd, D // 3, False)] * 3 + [(4 * r, FF // 2, False), (4 * r, FF // 2, True)] + [(4 * r, D, False)] + [(4 * r, 3 * D // 2, False)] * 2

    def bufs(f):
        return [VMEM(f(n, w, line), BF) for n, w, line in parts]

    bwd = pl.pallas_call(
        lambda *refs: backward_kernel(fold, T, D, FF, r, rd, refs),
        name="backward",
        out_shape=[shape((rows, Q, D)), shape((rows, Q, D)), shape((4, r, D), F32), shape((r, FF), F32), shape((rd, D), F32),
                   shape((VROWS, 128), F32)],
        in_specs=[vm_spec, vm_spec] + [any_spec] * len(saved),
        out_specs=[any_spec, any_spec, vm_spec, vm_spec, vm_spec, vm_spec],
        scratch_shapes=[
            VMEM((4, D, D), BF), VMEM((D, FF), BF), VMEM((T, D), BF), VMEM((3, T, D), BF), VMEM((T, D), BF),
            VMEM((6, 8, T), F32), VMEM((T, D), BF), VMEM((T, D), F32), VMEM((T, 128), F32), VMEM((T, FF), BF),
            VMEM((T, FF), BF), VMEM((T, D), F32), VMEM((T, D), BF), VMEM((VROWS, D), F32), VMEM((VROWS, D), F32),
            VMEM((T, D), BF), VMEM((T, D), BF), VMEM((3, T, D), BF),
        ] + [VMEM((2, 2) + parts[i][:2], BF) for i in (0, 1, 3, 5, 6)]
        + bufs(lambda n, w, line: (2, 2, n, w)) + bufs(lambda n, w, line: (2, 2, n, w))
        + bufs(lambda n, w, line: (2, 2, n // 2, w)) + bufs(lambda n, w, line: (2, n // 2, w))
        + bufs(lambda n, w, line: (4, n // 4, w)) + bufs(lambda n, w, line: (5 if line else 3, n // 4, w)) + [
            VMEM((4, VROWS, D), F32), VMEM((6, VROWS, D), F32),
        ] + sems,
        compiler_params=pltpu.CompilerParams(collective_id=1, has_side_effects=True, vmem_limit_bytes=61 * 2**20),
    )
    reduced = bwd(segment_ids, pad_mask, *kept)

    def line_of(n):
        return shape((1, n), F32)

    done = pl.pallas_call(
        finish_kernel,
        name="finish",
        out_shape=[shape((rows, Q, D)), shape((rows, Q, D))] + [shape((r, D), F32)] * 4 + [shape((r, FF), F32), shape((rd, D), F32)]
        + [line_of(r)] * 5 + [line_of(4 * r)] + [line_of(r)] * 3,
        in_specs=[any_spec] * 5 + [vm_spec],
        out_specs=[any_spec] * 8 + [vm_spec] * 9,
        scratch_shapes=[VMEM((rows, Q, D), BF), VMEM((rows, Q, D), BF), VMEM((4, r, D), F32), VMEM((r, FF), F32), VMEM((rd, D), F32),
                        pltpu.SemaphoreType.DMA((13,))],
        compiler_params=pltpu.CompilerParams(vmem_limit_bytes=60 * 2**20),
    )(*reduced)
    block_out, grad_in, gq, gk, gvv, go, gu, gd = done[:8]
    bq, bv, bo, ga, sa, bu, bd, gf, sf = [v.reshape(-1) for v in done[8:]]
    grads = [gq, bq, gk, gvv, bv, go, bo, ga, sa, gu, bu, gd, bd, gf, sf]
    if fold > 1:
        def narrow(g):
            n = g.shape[0]
            whole = jnp.zeros((32 * n,) + g.shape[1:], F32)
            whole = lax.dynamic_update_slice_in_dim(whole, g, part * n, 0)
            return lax.psum_scatter(whole, ("batch", "seq"), scatter_dimension=0, tiled=True)
        grads = [narrow(g) for g in grads]
    return (block_out, grad_in) + tuple(grads)


def solution(mesh):
    fold = mesh.shape["batch"] // 8
    mat, vec = P(("batch", "seq"), None), P(("batch", "seq"))
    act, rows = P("batch", "seq", None), P("batch", None)
    kinds = [mat, vec, mat, mat, vec, mat, vec, vec, vec, mat, vec, mat, vec, vec, vec]
    return jax.shard_map(
        lambda *args: per_device(fold, *args),
        mesh=mesh,
        in_specs=tuple([act, rows, rows, act] + kinds),
        out_specs=tuple([act, act] + kinds),
        check_vma=False,
    )
```

profile of v0, /device:TPU:0, one launch (start us, length us, event | category | flops | bytes accessed | tf_op | source)
XLA Modules:
  0.0 199.1 jit_solution(17617380192569832802)
XLA Ops:
  0.7 98.6 %forward.1 = (bf16[512,768]{1,0:T(8,128)(2,1)}, bf16[3,512,768]{2,1,0:T(8,128)(2,1)}, bf16[512,768]{1,0:T(8,128)(2,1)}, f32[6,8,512]{2,1,0:T(8,128)}, bf16[512,7...) custom-call(bf16[4,128,768]{2,1,0:T(8,128)(2,1)} %refs_0_.2, ...), custom_call_target="tpu_custom_call" | custom-call | tf_op jit(solution)/shard_map/forward/pallas_call | solution.py:903
  99.3 95.7 %backward.1 = (bf16[4,128,768]{2,1,0:T(8,128)(2,1)}, bf16[4,128,768]{2,1,0:T(8,128)(2,1)}, f32[4,24,768]{2,1,0:T(8,128)}, f32[24,3072]{1,0:T(8,128)}, f32[96,768]{1,0:T(8,128)}, /*index=5*/f32[16,128]{1,0:T(8,128)}) custom-call(s32[4,512]{1,0:T(4,128)} %refs_0_.3, s32[4,512]{1,0:T(4,128)} %refs_1_.3, bf16[512,768]{1,0:T(8,128)(2,1)} %get-tuple-element.57.refs_2_, ...), custom_call_target="tpu_custom_call" | custom-call | tf_op jit(solution)/shard_map/backward/pallas_call | solution.py:930
  195.0 3.9 %finish.1 = (bf16[4,128,768]{2,1,0:T(8,128)(2,1)}, bf16[4,128,768]{2,1,0:T(8,128)(2,1)}, f32[24,768]{1,0:T(8,128)}, f32[24,768]{1,0:T(8,128)}, f32[24,768]{1,0:T...) custom-call(bf16[4,128,768]{2,1,0:T(8,128)(2,1)} %get-tuple-element., ...), custom_call_target="tpu_custom_call" | custom-call | tf_op jit(solution)/shard_map/finish/pallas_call | solution.py:935
where the time goes:
time: 199 us
  Pallas kernels  198 us (99%)
    pallas_call x1, Pallas kernels, per_device(): fwd(hidden_in, cotangent, segment_ids, pad_mask, wq, wk, wv, wo, wu, wd,...  98.6 us
    pallas_call x1, Pallas kernels, per_device(): reduced = bwd(segment_ids, pad_mask, *kept)  95.7 us

commit v1 on v0

--- a/solution.py
+++ b/solution.py
@@ -322,23 +322,20 @@
         zero = jnp.zeros_like(v)
         v0_, v1_ = jnp.where(lo, v, one), jnp.where(lo, one, v)
         k0, k1 = jnp.where(lo, k, zero), jnp.where(lo, zero, k)
-        for step in range(T // 128):
-            rows = slice(step * 128, (step + 1) * 128)
-            q = qkv[0, rows, o]
-            ok = seg_col[rows] == key_row
-            res, top = [], []
-            for kk, vv in ((k0, v0_), (k1, v1_)):
-                s = jnp.where(ok, dg(q, kk, NT), NEG)
-                m = jnp.max(s, axis=-1, keepdims=True)
-                res.append(dg(jnp.exp(s - m).astype(BF), vv, NN))
-                top.append(m)
-            low = lo[:128]
-            num = jnp.where(low, res[0], res[1])
-            den = pltpu.roll(jnp.where(low, res[1], res[0]), 64, 1)
-            att[rows, o] = (num / den).astype(BF)
-            lt = (jnp.log(den) + jnp.where(low, top[0], top[1])).T
-            lse[p, 0:1, rows] = lt[0:1]
-            lse[p, 1:2, rows] = lt[64:65]
+        q = qkv[0, :, o]
+        ok = seg_col == key_row
+        res, top = [], []
+        for kk, vv in ((k0, v0_), (k1, v1_)):
+            s = jnp.where(ok, dg(q, kk, NT), NEG)
+            m = jnp.max(s, axis=-1, keepdims=True)
+            res.append(dg(jnp.exp(s - m).astype(BF), vv, NN))
+            top.append(m)
+        num = jnp.where(lo, res[0], res[1])
+        den = pltpu.roll(jnp.where(lo, res[1], res[0]), 64, 1)
+        att[:, o] = (num / den).astype(BF)
+        lt = (jnp.log(den) + jnp.where(lo, top[0], top[1])).T
+        lse[p, 0:1, :] = lt[0:1]
+        lse[p, 1:2, :] = lt[64:65]
 
     tags = {}
 
@@ -479,11 +476,7 @@
     def load(src, dst):
         return local.start(lambda: src, lambda: dst)
 
-    l_act, l_gffn, l_wD, l_gp = load(i_act, act), load(i_gffn, gffn), load(i_wD, w1), load(i_gp, gp)
-    l_gvec, l_nlow, l_gmid, l_wU = load(i_gvec, gvec), load(i_nlow, nlow), load(i_gmid, gmid), load(i_wU, wU)
-    l_vec, l_xh1, l_inv1, l_att = load(i_vec, vec), load(i_xh1, xh1), load(i_inv1, inv1), load(i_att, att)
-    l_qkv, l_lse, l_tok = load(i_qkv, qkv), load(i_lse, lse), load(i_tok, tok)
-    local.start(lambda: i_out.at[ds(z * Q, Q)], lambda: bout.at[z])
+    l_act, l_gffn = load(i_act, act), load(i_gffn, gffn)
     me.greet()
     t_out = [wire.send(lambda k=k: i_out.at[ds(me.zidx[k] * Q, Q)], lambda: bout.at[z], me.zdev[k]) for k in range(3)]
 
@@ -640,10 +633,15 @@
 
     local.wait(l_act)
     local.wait(l_gffn)
+    l_wD, l_gp = load(i_wD, w1), load(i_gp, gp)
     down_grad(D0, 0)
     D0.core()
+    l_gvec, l_nlow, l_gmid, l_wU = load(i_gvec, gvec), load(i_nlow, nlow), load(i_gmid, gmid), load(i_wU, wU)
     down_grad(D1, 1)
     D1.core()
+    l_vec, l_xh1, l_inv1, l_att = load(i_vec, vec), load(i_xh1, xh1), load(i_inv1, inv1), load(i_att, att)
+    l_qkv, l_lse, l_tok = load(i_qkv, qkv), load(i_lse, lse), load(i_tok, tok)
+    local.start(lambda: i_out.at[ds(z * Q, Q)], lambda: bout.at[z])
     D0.plane_one()
     wire.sent(D0.tc)
     down_grad(D2, 2)
@@ -709,13 +707,14 @@
         gm = (jnp.where(lo, g, zero), jnp.where(lo, zero, g))
         km = (jnp.where(lo, k, zero), jnp.where(lo, zero, k))
         dq = jnp.zeros((T, 128), F32)
-        for step in range(T // 128):
-            rows = slice(step * 128, (step + 1) * 128)
+        half = T // 2
+        for step in range(2):
+            rows = slice(step * half, (step + 1) * half)
             kc = qkv[1, rows, o]
             vc = qkv[2, rows, o]
             ok = key_col[rows] == seg_row
-            dk = jnp.zeros((128, 128), F32)
-            dv = jnp.zeros((128, 128), F32)
+            dk = jnp.zeros((half, 128), F32)
+            dv = jnp.zeros((half, 128), F32)
             for hh in range(2):
                 s = jnp.where(ok, dg(kc, qm[hh], NT), NEG)
                 pt = jnp.exp(s - lse[p, hh:hh + 1, :])
@@ -756,7 +755,7 @@
         D2.along()
 
     def serve5():
-        U1.plane_two()
+        pass
 
     services = [serve0, serve1, serve2, serve3, serve4, serve5]
 
@@ -766,15 +765,17 @@
         for i, service in enumerate(services):
             pl.when(p == i)(service)
 
-    gin = gattn
-    store(O, dg(att[...], gattn[...], TN), slice(0, D))
-    O.core()
-    U0.along()
+    gin = gatt
     gmid[...] += dg(gqkv[0], w1[0], NT)
     gmid[...] += dg(gqkv[1], w1[1], NT)
     gin[...] = (gmid[...] + dg(gqkv[2], w1[2], NT)).astype(BF)
     local.start(lambda: gin.at[ds(z * Q, Q)], lambda: gin_out.at[z])
     t_gin = [wire.send(lambda k=k: gin.at[ds(me.zidx[k] * Q, Q)], lambda: gin_out.at[z], me.zdev[k]) for k in range(3)]
+    U1.plane_two()
+    grad_o = dg(att[...], gattn[...], TN)
+    store(O, grad_o, slice(0, D))
+    O.core()
+    U0.along()
     O.plane_one()
     qkv_grad(A0, 0)
     A0.core()

time: 199 us -> 193 us (0.970)
  Pallas kernels: 198 us -> 192 us
    pallas_call x1, Pallas kernels: 95.7 us -> 92.1 us  [per_device(): reduced = bwd(segment_ids, pad_mask, *kept)]
    pallas_call x1, Pallas kernels: 98.6 us -> 96.2 us  [per_device(): fwd(hidden_in, cotangent, segment_ids, pad_mask, wq, wk, wv, wo, wu, wd,...]
where the time goes in v1:
time: 193 us
  Pallas kernels  192 us (99%)
    pallas_call x1, Pallas kernels, per_device(): fwd(hidden_in, cotangent, segment_ids, pad_mask, wq, wk, wv, wo, wu, wd,...  96.2 us
    pallas_call x1, Pallas kernels, per_device(): reduced = bwd(segment_ids, pad_mask, *kept)  92.1 us
    pallas_call x1, Pallas kernels, per_device(): pl.pallas_call(finish_kernel, name='finish', out_shape=[shape((rows, Q, D...  3.93 us

profile of v1, /device:TPU:0, one launch (start us, length us, event | category | flops | bytes accessed | tf_op | source)
XLA Modules:
  0.0 193.0 jit_solution(12678164470710043545)
XLA Ops:
  0.7 96.2 %forward.1 = (bf16[512,768]{1,0:T(8,128)(2,1)}, bf16[3,512,768]{2,1,0:T(8,128)(2,1)}, bf16[512,768]{1,0:T(8,128)(2,1)}, f32[6,8,512]{2,1,0:T(8,128)}, bf16[512,7...) custom-call(bf16[4,128,768]{2,1,0:T(8,128)(2,1)} %refs_0_.2, ...), custom_call_target="tpu_custom_call" | custom-call | tf_op jit(solution)/shard_map/forward/pallas_call | solution.py:904
  96.8 92.1 %backward.1 = (bf16[4,128,768]{2,1,0:T(8,128)(2,1)}, bf16[4,128,768]{2,1,0:T(8,128)(2,1)}, f32[4,24,768]{2,1,0:T(8,128)}, f32[24,3072]{1,0:T(8,128)}, f32[96,768]{1,0:T(8,128)}, /*index=5*/f32[16,128]{1,0:T(8,128)}) custom-call(s32[4,512]{1,0:T(4,128)} %refs_0_.3, s32[4,512]{1,0:T(4,128)} %refs_1_.3, bf16[512,768]{1,0:T(8,128)(2,1)} %get-tuple-element.57.refs_2_, ...), custom_call_target="tpu_custom_call" | custom-call | tf_op jit(solution)/shard_map/backward/pallas_call | solution.py:931
  188.9 3.9 %finish.1 = (bf16[4,128,768]{2,1,0:T(8,128)(2,1)}, bf16[4,128,768]{2,1,0:T(8,128)(2,1)}, f32[24,768]{1,0:T(8,128)}, f32[24,768]{1,0:T(8,128)}, f32[24,768]{1,0:T...) custom-call(bf16[4,128,768]{2,1,0:T(8,128)(2,1)} %get-tuple-element., ...), custom_call_target="tpu_custom_call" | custom-call | tf_op jit(solution)/shard_map/finish/pallas_call | solution.py:936
